TPU v7x, 32 devices: a whole 2x2x4 slice. The times are simulated.
32 devices in a mesh: cp: 16 (over z, y, x), tp: 2 (over core).
Axes of the slice: x: 2, y: 2, z: 4, core: 2. Of those that a mesh axis runs over, the one named last changes fastest.
Arguments:
- hidden_states: bfloat16 [2048, 4096], P('cp', 'tp'), may hold values from -18 to 18
- query: bfloat16 [2048, 4096], P('cp', 'tp'), may hold values from -300 to 300
- attention_output_gradient: bfloat16 [2048, 4096], P('cp', 'tp'), may hold values from -6 to 6
- key_weight: bfloat16 [4096, 512], P('cp', 'tp'), may hold values from -0.09375 to 0.09375
- value_projection_weight: bfloat16 [4096, 512], P('cp', 'tp'), may hold values from -0.09375 to 0.09375
- doc_start: int32 [2048], P('cp'), may hold values from 0 to 2047, as said below
Outputs:
- grad_query: bfloat16 [2048, 4096], P('cp', 'tp')
- grad_hidden: bfloat16 [2048, 4096], P('cp')
- grad_key_weight: float32 [4096, 512], P('cp', 'tp')
- grad_value_weight: float32 [4096, 512], P('cp', 'tp')
Inputs may be any that keep to these rules, and one draw needn't show every extreme that they name: `doc_start`: each entry is the position of the first token of that token's document; documents are runs of consecutive tokens; no document holds tokens on both sides of a multiple of 1024; one document has exactly 1024 tokens; the last token is a document of its own.
All inputs are finite; a program needn't handle non-finite values.
Results may differ from a plain program's by a relative error of at most 0.0071.
Values may be sent and summed in bfloat16 or wider, within the bound.
A program may use at most 64 MiB of HBM per device.

v0:
```python
import jax
import jax.numpy as jnp
from jax import lax
from jax.sharding import PartitionSpec as P

HEAD_SIZE = 128
SPAN = 8


NEG_FILL = -1e30


def passed_along(value, axis, steps):
    count = lax.axis_size(axis)
    leading, last = (max(0, -steps), min(count, count - steps))
    return lax.ppermute(value, axis, [(source, source + steps) for source in range(leading, last)])


def from_behind(block, axis, distance):
    devices = range(lax.axis_size(axis))
    route = [((i - distance) % len(devices), i) for i in devices]
    return lax.ppermute(block, axis, route)


def split_pair(kv_block, heads_kv):
    row_count = kv_block.shape[0]
    kv_width = kv_block.shape[1] // 2
    key_part = kv_block[:, :kv_width].reshape(row_count, heads_kv, HEAD_SIZE)
    value_part = kv_block[:, kv_width:].reshape(row_count, heads_kv, HEAD_SIZE)
    return (key_part, value_part)


def forward_tile(running, query_heads, kv_block, visible_now, inv_sqrt):
    row_max, row_total, weighted = running
    key_part, value_part = split_pair(kv_block, query_heads.shape[1])
    scores = (
        jnp.einsum("qgrd,kgd->grqk", query_heads, key_part, preferred_element_type=jnp.float32)
        * inv_sqrt
    )
    scores = jnp.where(visible_now, scores, NEG_FILL)
    new_max = jnp.maximum(row_max, jnp.max(scores, axis=-1))
    probs_now = jnp.where(visible_now, jnp.exp(scores - new_max[..., None]), 0.0)
    fading = jnp.exp(row_max - new_max)
    new_total = row_total * fading + jnp.sum(probs_now, axis=-1)
    added = jnp.einsum(
        "grqk,kgd->grqd", probs_now, value_part.astype(jnp.float32), precision=lax.Precision.HIGHEST
    )
    return (new_max, new_total, weighted * fading[..., None] + added)


def backward_tile(query_heads, grad_heads, log_total, delta_rows, kv_block, visible_now, inv_sqrt):
    row_count = query_heads.shape[0]
    key_part, value_part = split_pair(kv_block, query_heads.shape[1])
    scores = (
        jnp.einsum("qgrd,kgd->grqk", query_heads, key_part, preferred_element_type=jnp.float32)
        * inv_sqrt
    )
    scores = jnp.where(visible_now, scores, NEG_FILL)
    probs_now = jnp.where(visible_now, jnp.exp(scores - log_total[..., None]), 0.0)
    value_gradient_total = jnp.einsum(
        "grqk,qgrd->kgd",
        probs_now.astype(jnp.bfloat16),
        grad_heads,
        preferred_element_type=jnp.float32,
    )
    prob_grad = jnp.einsum(
        "qgrd,kgd->grqk", grad_heads, value_part, preferred_element_type=jnp.float32
    )
    score_grad = (probs_now * (prob_grad - delta_rows[..., None])).astype(jnp.bfloat16)
    query_grad = (
        jnp.einsum("grqk,kgd->qgrd", score_grad, key_part, preferred_element_type=jnp.float32)
        * inv_sqrt
    )
    key_gradient_total = (
        jnp.einsum("grqk,qgrd->kgd", score_grad, query_heads, preferred_element_type=jnp.float32)
        * inv_sqrt
    )
    paired_gradient = jnp.concatenate(
        [key_gradient_total.reshape(row_count, -1), value_gradient_total.reshape(row_count, -1)],
        axis=1,
    )
    return (query_grad.reshape(row_count, -1), paired_gradient)


def per_device(
    hidden_states, query, attention_output_gradient, key_weight, value_projection_weight, doc_start
):
    row_count = query.shape[0]
    node_count = lax.axis_size("cp")
    my_index = lax.axis_index("cp")
    chain_len = min(SPAN, node_count // 2)
    kv_width = key_weight.shape[1]
    heads_kv = kv_width // HEAD_SIZE
    query_per_key_heads = query.shape[1] // kv_width
    inv_sqrt = HEAD_SIZE ** (-0.5)
    features = lax.all_gather(hidden_states, "tp", axis=1, tiled=True)
    key_full, value_full = (
        lax.all_gather(key_weight, "cp", axis=0, tiled=True),
        lax.all_gather(value_projection_weight, "cp", axis=0, tiled=True),
    )
    key_rows = jnp.dot(features, key_full, preferred_element_type=jnp.float32).astype(jnp.bfloat16)
    value_rows = jnp.dot(features, value_full, preferred_element_type=jnp.float32).astype(
        jnp.bfloat16
    )
    local_block = jnp.concatenate([key_rows, value_rows], axis=1)
    query_heads = query.reshape(row_count, heads_kv, query_per_key_heads, HEAD_SIZE)
    grad_heads = attention_output_gradient.reshape(
        row_count, heads_kv, query_per_key_heads, HEAD_SIZE
    )
    offsets = jnp.arange(row_count, dtype=jnp.int32)
    query_pos = my_index * row_count + offsets

    def visible(turn_index):
        source = my_index - turn_index
        key_pos = source * row_count + offsets
        return (
            (key_pos[None, :] >= doc_start[:, None])
            & (key_pos[None, :] <= query_pos[:, None])
            & (source >= 0)
        )

    start_stats = (
        jnp.full((heads_kv, query_per_key_heads, row_count), NEG_FILL, jnp.float32),
        jnp.zeros((heads_kv, query_per_key_heads, row_count), jnp.float32),
        jnp.zeros((heads_kv, query_per_key_heads, row_count, HEAD_SIZE), jnp.float32),
    )
    running = forward_tile(start_stats, query_heads, local_block, visible(0), inv_sqrt)
    stored = jnp.zeros((1,), jnp.bfloat16)

    def forward_turn(turn_index, carried):
        kv_block, stats_now, stored_now = carried
        kv_block = passed_along(kv_block, "cp", 1)
        visible_now = visible(turn_index)
        stats_now = lax.cond(
            jnp.any(visible_now),
            lambda: forward_tile(stats_now, query_heads, kv_block, visible_now, inv_sqrt),
            lambda: stats_now,
        )
        return (kv_block, stats_now, stored_now)

    unused_block, running, stored = lax.fori_loop(
        1, chain_len, forward_turn, (local_block, running, stored)
    )
    row_max, row_total, weighted = running
    log_total = row_max + jnp.log(row_total)
    attended = weighted / row_total[..., None]
    delta_rows = jnp.einsum(
        "qgrd,grqd->grq", grad_heads.astype(jnp.float32), attended, precision=lax.Precision.HIGHEST
    )
    query_sum, kv_sums = backward_tile(
        query_heads, grad_heads, log_total, delta_rows, local_block, visible(0), inv_sqrt
    )

    def backward_turn(turn_index, carried):
        kv_block, sums_now, query_now = carried
        sums_now = from_behind(sums_now, "cp", 1)
        kv_block = passed_along(kv_block, "cp", 1)
        visible_now = visible(turn_index)
        query_part, pair_part = lax.cond(
            jnp.any(visible_now),
            lambda: backward_tile(
                query_heads, grad_heads, log_total, delta_rows, kv_block, visible_now, inv_sqrt
            ),
            lambda: (jnp.zeros_like(query_now), jnp.zeros_like(sums_now)),
        )
        return (kv_block, sums_now + pair_part, query_now + query_part)

    unused_last, kv_sums, query_sum = lax.fori_loop(
        1, chain_len, backward_turn, (local_block, kv_sums, query_sum)
    )
    returned = from_behind(kv_sums.astype(jnp.bfloat16), "cp", 1 - chain_len).astype(kv_sums.dtype)
    gradients_lowered = returned.astype(jnp.bfloat16)
    weight_sums = lax.psum_scatter(
        lax.dot_general(
            features,
            gradients_lowered,
            (((0,), (0,)), ((), ())),
            preferred_element_type=jnp.float32,
        ),
        "cp",
        scatter_dimension=0,
        tiled=True,
    )
    projection = jnp.concatenate([key_full, value_full], axis=1)
    input_part = lax.dot_general(
        gradients_lowered, projection, (((1,), (1,)), ((), ())), preferred_element_type=jnp.float32
    )
    grad_hidden = lax.psum(input_part, "tp").astype(jnp.bfloat16)
    return (
        query_sum.astype(jnp.bfloat16),
        grad_hidden,
        weight_sums[:, :kv_width],
        weight_sums[:, kv_width:],
    )


def solution(mesh):
    return jax.shard_map(
        per_device,
        mesh=mesh,
        in_specs=(
            P("cp", "tp"),
            P("cp", "tp"),
            P("cp", "tp"),
            P("cp", "tp"),
            P("cp", "tp"),
            P("cp"),
        ),
        out_specs=(P("cp", "tp"), P("cp", None), P("cp", "tp"), P("cp", "tp")),
        check_vma=False,
    )
```

profile of v0, /device:TPU:0, one launch (start us, length us, event | category | flops | bytes accessed | tf_op | source)
XLA Modules:
  0.0 538.9 jit_solution(3174974900019219948)
XLA Ops:
  9.4 1.3 copy.50
  12.1 9.2 %all-gather.4.cloned.1.call-done = bf16[128,4096]{1,0:T(8,128)(2,1)} async-done(((bf16[128,2048]{1,0:T(8,128)(2,1)}), bf16[128,4096]{1,0:T(8,128)(2,1)}) %all-gather.4.cloned.1.call-update) | async-done | bytes 1048592 | tf_op jit(solution)/shard_map/all_gather | solution.py:96
  21.3 64.7 %all-gather.6.cloned.1.call-done = bf16[4096,256]{1,0:T(8,128)(2,1)} async-done(((bf16[256,256]{1,0:T(8,128)(2,1)}), bf16[4096,256]{1,0:T(8,128)(2,1)}) %all-gather.6.cloned.1.call-update) | async-done | bytes 2097168 | tf_op jit(solution)/shard_map/all_gather | solution.py:98
  86.0 2.4 convolution_convert_fusion.1
  88.4 59.8 %all-gather.8.cloned.1.call-done = bf16[4096,256]{1,0:T(8,128)(2,1)} async-done(((bf16[256,256]{1,0:T(8,128)(2,1)}), bf16[4096,256]{1,0:T(8,128)(2,1)}) %all-gather.8.cloned.1.call-update) | async-done | bytes 2097168 | tf_op jit(solution)/shard_map/all_gather | solution.py:99
  148.2 2.0 convolution_convert_fusion
  153.0 55.7 %while.38 = (s32[]{:T(128)}, bf16[128,512]{0,1:T(8,128)(2,1)S(1)}, f32[2,8,128]{2,1,0:T(8,128)S(1)}, f32[2,8,128]{2,1,0:T(8,128)S(1)}, f32[2,8,128,128]{3,2,1,0:...) while((s32[]{:T(128)}, bf16[128,512]{0,1:T(8,128)(2,1)S(1)}, ...), condition=%wide.region_8.9_spmd.clone, body=%wide.region_2.8_spmd.clone.sunk | while | flops 472469760 | bytes 7146293 | solution.py:141
  153.1 3.2 collective-permute-start
  156.3 1.4 and_and_fusion.5
  158.8 6.3 %collective-permute-start = (bf16[128,512]{0,1:T(8,128)(2,1)S(1)}, bf16[128,512]{0,1:T(8,128)(2,1)S(1)}, u32[]{:S(2)}, u32[]{:S(2)}) collective-permute-start(bf16[128,512]{0,1:T(8,128)(2,1)S(1)} %get-tuple-element.744), channel_id=1, source_target_pairs={{0,2},{2,4},{4,6},{6,8},{8,10},{10,12},{12,14},{14,16},{16,18},{18... | collective-permute-start | bytes 393224 | tf_op jit(solution)/shard_map/while/body/eval_jaxpr/ppermute | solution.py:16
  165.2 1.4 and_and_fusion.5
  167.6 4.5 collective-permute-start
  172.2 1.4 and_and_fusion.5
  174.7 7.2 %collective-permute-start = (bf16[128,512]{0,1:T(8,128)(2,1)S(1)}, bf16[128,512]{0,1:T(8,128)(2,1)S(1)}, u32[]{:S(2)}, u32[]{:S(2)}) collective-permute-start(bf16[128,512]{0,1:T(8,128)(2,1)S(1)} %get-tuple-element.744), channel_id=1, source_target_pairs={{0,2},{2,4},{4,6},{6,8},{8,10},{10,12},{12,14},{14,16},{16,18},{18... | collective-permute-start | bytes 393224 | tf_op jit(solution)/shard_map/while/body/eval_jaxpr/ppermute | solution.py:16
  181.9 1.4 and_and_fusion.5
  184.4 5.3 collective-permute-start
  189.7 1.4 and_and_fusion.5
  192.2 5.3 collective-permute-start
  197.6 1.4 and_and_fusion.5
  200.1 6.2 %collective-permute-start = (bf16[128,512]{0,1:T(8,128)(2,1)S(1)}, bf16[128,512]{0,1:T(8,128)(2,1)S(1)}, u32[]{:S(2)}, u32[]{:S(2)}) collective-permute-start(bf16[128,512]{0,1:T(8,128)(2,1)S(1)} %get-tuple-element.744), channel_id=1, source_target_pairs={{0,2},{2,4},{4,6},{6,8},{8,10},{10,12},{12,14},{14,16},{16,18},{18... | collective-permute-start | bytes 393224 | tf_op jit(solution)/shard_map/while/body/eval_jaxpr/ppermute | solution.py:16
  206.3 1.4 and_and_fusion.5
  208.8 1.3 broadcast_divide_fusion
  210.7 1.6 copy.84
  215.8 119.5 %while.39 = (s32[]{:T(128)}, bf16[128,512]{0,1:T(8,128)(2,1)S(1)}, f32[128,512]{0,1:T(8,128)}, f32[128,2048]{0,1:T(8,128)S(1)}, s32[]{:T(128)}, /*index=5*/s32[1...) while((s32[]{:T(128)}, bf16[128,512]{0,1:T(8,128)(2,1)S(1)}, ...), condition=%wide.region_13.14_spmd.clone, body=%wide.region_9.13_spmd.clone.sunk | while | flops 338411776 | bytes 14961505 | solution.py:168
  215.8 9.4 %collective-permute-start.1 = (bf16[128,512]{0,1:T(8,128)(2,1)S(1)}, bf16[128,512]{0,1:T(8,128)(2,1)S(1)}, u32[]{:S(2)}, u32[]{:S(2)}) collective-permute-start(bf16[128,512]{0,1:T(8,128)(2,1)S(1)} %get-tuple-element.782), channel_id=1, source_target_pairs={{0,2},{2,4},{4,6},{6,8},{8,10},{10,12},{12,14},{14,16},{16,18},{18... | collective-permute-start | bytes 393224 | tf_op jit(solution)/shard_map/while/body/eval_jaxpr/ppermute | solution.py:16
  225.2 4.5 collective-permute-start.2
  229.8 1.4 and_and_fusion.6
  232.2 3.8 collective-permute-done.2
  236.0 1.7 add.182
  237.6 4.8 collective-permute-start.1
  242.4 5.1 collective-permute-start.2
  247.6 1.4 and_and_fusion.6
  250.0 3.7 collective-permute-done.2
  253.7 1.7 add.182
  255.4 5.0 collective-permute-start.1
  260.4 3.4 collective-permute-start.2
  263.8 1.4 and_and_fusion.6
  266.2 6.5 %collective-permute-done.2 = f32[128,512]{0,1:T(8,128)} collective-permute-done((f32[128,512]{0,1:T(8,128)}, f32[128,512]{0,1:T(8,128)}, u32[]{:S(2)}, u32[]{:S(2)}) %collective-permute-start.2) | collective-permute-done | bytes 262176 | tf_op jit(solution)/shard_map/while/body/eval_jaxpr/ppermute | solution.py:22
  272.7 1.7 add.182
  274.4 1.7 collective-permute-start.1
  276.1 3.5 collective-permute-start.2
  279.6 1.4 and_and_fusion.6
  282.0 5.9 %collective-permute-done.2 = f32[128,512]{0,1:T(8,128)} collective-permute-done((f32[128,512]{0,1:T(8,128)}, f32[128,512]{0,1:T(8,128)}, u32[]{:S(2)}, u32[]{:S(2)}) %collective-permute-start.2) | collective-permute-done | bytes 262176 | tf_op jit(solution)/shard_map/while/body/eval_jaxpr/ppermute | solution.py:22
  287.8 1.7 add.182
  289.5 2.4 collective-permute-start.1
  291.9 3.8 collective-permute-start.2
  295.7 1.4 and_and_fusion.6
  298.1 5.2 collective-permute-done.2
  303.3 1.7 add.182
  305.0 2.5 collective-permute-start.1
  307.4 4.1 collective-permute-start.2
  311.5 1.4 and_and_fusion.6
  313.9 3.8 collective-permute-done.2
  317.8 1.7 add.182
  319.4 3.8 collective-permute-start.1
  323.2 3.4 collective-permute-start.2
  326.7 1.4 and_and_fusion.6
  329.1 4.6 collective-permute-done.2
  333.7 1.7 add.182
  336.4 6.8 %collective-permute-done.3 = bf16[128,512]{0,1:T(8,128)(2,1)S(1)} collective-permute-done((bf16[128,512]{0,1:T(8,128)(2,1)S(1)}, bf16[128,512]{0,1:T(8,128)(2,1)S(1)}, u32[]{:S(2)}, u32[]{:S(2)}) %collective-permute-start.3) | collective-permute-done | bytes 131104 | tf_op jit(solution)/shard_map/ppermute | solution.py:22
  343.1 5.7 %convolution_bitcast_fusion.2 = f32[4096,512]{0,1:T(8,128)} fusion(bf16[128,512]{0,1:T(8,128)(2,1)S(1)} %collective-permute-done.3, bf16[128,4096]{1,0:T(8,128)(2,1)} %all-gather.4.cloned.1.call-done), kind=kOutput, calls=%fused_computation.40 | convolution fusion | flops 536870912 | bytes 9568256 | tf_op jit(solution)/shard_map/dot_general | solution.py:174
  349.8 3.7 fusion.28
  353.6 9.3 %all-reduce.1 = bf16[128,4096]{1,0:T(8,128)(2,1)} all-reduce(f32[128,4096]{1,0:T(8,128)S(1)} %fusion.28), channel_id=1, replica_groups=mesh['cp'=16,'tp'=2] {'tp'}, use_global_device_ids=true, to_apply=%region_14.15 | all-reduce | flops 524288 | bytes 3145728 | tf_op jit(solution)/shard_map/psum | solution.py:188
  362.8 166.8 %reduce-scatter.2.cloned.1.call-done = f32[256,512]{0,1:T(8,128)} async-done(((f32[4096,512]{0,1:T(8,128)}), f32[256,512]{0,1:T(8,128)}) %reduce-scatter.2.cloned.1.call-update) | async-done | bytes 524304 | tf_op jit(solution)/shard_map/reduce_scatter | solution.py:173
  (137 shorter events, 21.5 us)
Async XLA Ops:
  7.2 3.6 copy-start.3
  7.2 14.1 %all-gather.4.cloned.1.call-start = ((), (), s32[]{:S(2)}) async-start(), calls=%async_computation.1 | async-start | bytes 1572864 | tf_op jit(solution)/shard_map/all_gather | solution.py:96
  7.9 78.1 %all-gather.6.cloned.1.call-start = ((), (), s32[]{:S(2)}) async-start(), calls=%async_computation.2 | async-start | bytes 2228224 | tf_op jit(solution)/shard_map/all_gather | solution.py:98
  8.7 139.5 %all-gather.8.cloned.1.call-start = ((), (), s32[]{:S(2)}) async-start(), calls=%async_computation.3 | async-start | bytes 2228224 | tf_op jit(solution)/shard_map/all_gather | solution.py:99
  9.4 520.3 %reduce-scatter.2.cloned.1.call-start = ((), (), s32[]{:S(2)}) async-start(), calls=%async_computation.4 | async-start | bytes 8912896 | tf_op jit(solution)/shard_map/reduce_scatter | solution.py:173
  21.3 126.8 %copy-start.2 = (bf16[128,4096]{1,0:T(8,128)(2,1)S(1)}, bf16[128,4096]{1,0:T(8,128)(2,1)}, u32[]{:S(2)}) copy-start(bf16[128,4096]{1,0:T(8,128)(2,1)} %all-gather.4.cloned.1.call-done) | copy-start | bytes 3145732
  150.9 1.0 copy-start
  153.1 5.7 %collective-permute-start = (bf16[128,512]{0,1:T(8,128)(2,1)S(1)}, bf16[128,512]{0,1:T(8,128)(2,1)S(1)}, u32[]{:S(2)}, u32[]{:S(2)}) collective-permute-start(bf16[128,512]{0,1:T(8,128)(2,1)S(1)} %get-tuple-element.744), channel_id=1, source_target_pairs={{0,2},{2,4},{4,6},{6,8},{8,10},{10,12},{12,14},{14,16},{16,18},{18... | collective-permute-start | bytes 393224 | tf_op jit(solution)/shard_map/while/body/eval_jaxpr/ppermute | solution.py:16
  158.8 8.8 %collective-permute-start = (bf16[128,512]{0,1:T(8,128)(2,1)S(1)}, bf16[128,512]{0,1:T(8,128)(2,1)S(1)}, u32[]{:S(2)}, u32[]{:S(2)}) collective-permute-start(bf16[128,512]{0,1:T(8,128)(2,1)S(1)} %get-tuple-element.744), channel_id=1, source_target_pairs={{0,2},{2,4},{4,6},{6,8},{8,10},{10,12},{12,14},{14,16},{16,18},{18... | collective-permute-start | bytes 393224 | tf_op jit(solution)/shard_map/while/body/eval_jaxpr/ppermute | solution.py:16
  167.6 7.0 %collective-permute-start = (bf16[128,512]{0,1:T(8,128)(2,1)S(1)}, bf16[128,512]{0,1:T(8,128)(2,1)S(1)}, u32[]{:S(2)}, u32[]{:S(2)}) collective-permute-start(bf16[128,512]{0,1:T(8,128)(2,1)S(1)} %get-tuple-element.744), channel_id=1, source_target_pairs={{0,2},{2,4},{4,6},{6,8},{8,10},{10,12},{12,14},{14,16},{16,18},{18... | collective-permute-start | bytes 393224 | tf_op jit(solution)/shard_map/while/body/eval_jaxpr/ppermute | solution.py:16
  174.7 9.7 %collective-permute-start = (bf16[128,512]{0,1:T(8,128)(2,1)S(1)}, bf16[128,512]{0,1:T(8,128)(2,1)S(1)}, u32[]{:S(2)}, u32[]{:S(2)}) collective-permute-start(bf16[128,512]{0,1:T(8,128)(2,1)S(1)} %get-tuple-element.744), channel_id=1, source_target_pairs={{0,2},{2,4},{4,6},{6,8},{8,10},{10,12},{12,14},{14,16},{16,18},{18... | collective-permute-start | bytes 393224 | tf_op jit(solution)/shard_map/while/body/eval_jaxpr/ppermute | solution.py:16
  184.4 7.8 %collective-permute-start = (bf16[128,512]{0,1:T(8,128)(2,1)S(1)}, bf16[128,512]{0,1:T(8,128)(2,1)S(1)}, u32[]{:S(2)}, u32[]{:S(2)}) collective-permute-start(bf16[128,512]{0,1:T(8,128)(2,1)S(1)} %get-tuple-element.744), channel_id=1, source_target_pairs={{0,2},{2,4},{4,6},{6,8},{8,10},{10,12},{12,14},{14,16},{16,18},{18... | collective-permute-start | bytes 393224 | tf_op jit(solution)/shard_map/while/body/eval_jaxpr/ppermute | solution.py:16
  192.2 7.8 %collective-permute-start = (bf16[128,512]{0,1:T(8,128)(2,1)S(1)}, bf16[128,512]{0,1:T(8,128)(2,1)S(1)}, u32[]{:S(2)}, u32[]{:S(2)}) collective-permute-start(bf16[128,512]{0,1:T(8,128)(2,1)S(1)} %get-tuple-element.744), channel_id=1, source_target_pairs={{0,2},{2,4},{4,6},{6,8},{8,10},{10,12},{12,14},{14,16},{16,18},{18... | collective-permute-start | bytes 393224 | tf_op jit(solution)/shard_map/while/body/eval_jaxpr/ppermute | solution.py:16
  200.1 8.7 %collective-permute-start = (bf16[128,512]{0,1:T(8,128)(2,1)S(1)}, bf16[128,512]{0,1:T(8,128)(2,1)S(1)}, u32[]{:S(2)}, u32[]{:S(2)}) collective-permute-start(bf16[128,512]{0,1:T(8,128)(2,1)S(1)} %get-tuple-element.744), channel_id=1, source_target_pairs={{0,2},{2,4},{4,6},{6,8},{8,10},{10,12},{12,14},{14,16},{16,18},{18... | collective-permute-start | bytes 393224 | tf_op jit(solution)/shard_map/while/body/eval_jaxpr/ppermute | solution.py:16
  210.1 2.3 copy-start.1
  212.4 2.4 copy-start.4
  215.8 16.0 %collective-permute-start.1 = (bf16[128,512]{0,1:T(8,128)(2,1)S(1)}, bf16[128,512]{0,1:T(8,128)(2,1)S(1)}, u32[]{:S(2)}, u32[]{:S(2)}) collective-permute-start(bf16[128,512]{0,1:T(8,128)(2,1)S(1)} %get-tuple-element.782), channel_id=1, source_target_pairs={{0,2},{2,4},{4,6},{6,8},{8,10},{10,12},{12,14},{14,16},{16,18},{18... | collective-permute-start | bytes 393224 | tf_op jit(solution)/shard_map/while/body/eval_jaxpr/ppermute | solution.py:16
  225.2 10.7 %collective-permute-start.2 = (f32[128,512]{0,1:T(8,128)}, f32[128,512]{0,1:T(8,128)}, u32[]{:S(2)}, u32[]{:S(2)}) collective-permute-start(f32[128,512]{0,1:T(8,128)} %get-tuple-element.783), channel_id=1, source_target_pairs={{30,0},{0,2},{2,4},{4,6},{6,8},{8,10},{10,12},{12,14},{14,16},{16,... | collective-permute-start | bytes 786440 | tf_op jit(solution)/shard_map/while/body/eval_jaxpr/ppermute | solution.py:22
  237.6 11.9 %collective-permute-start.1 = (bf16[128,512]{0,1:T(8,128)(2,1)S(1)}, bf16[128,512]{0,1:T(8,128)(2,1)S(1)}, u32[]{:S(2)}, u32[]{:S(2)}) collective-permute-start(bf16[128,512]{0,1:T(8,128)(2,1)S(1)} %get-tuple-element.782), channel_id=1, source_target_pairs={{0,2},{2,4},{4,6},{6,8},{8,10},{10,12},{12,14},{14,16},{16,18},{18... | collective-permute-start | bytes 393224 | tf_op jit(solution)/shard_map/while/body/eval_jaxpr/ppermute | solution.py:16
  242.4 11.3 %collective-permute-start.2 = (f32[128,512]{0,1:T(8,128)}, f32[128,512]{0,1:T(8,128)}, u32[]{:S(2)}, u32[]{:S(2)}) collective-permute-start(f32[128,512]{0,1:T(8,128)} %get-tuple-element.783), channel_id=1, source_target_pairs={{30,0},{0,2},{2,4},{4,6},{6,8},{8,10},{10,12},{12,14},{14,16},{16,... | collective-permute-start | bytes 786440 | tf_op jit(solution)/shard_map/while/body/eval_jaxpr/ppermute | solution.py:22
  255.4 10.5 %collective-permute-start.1 = (bf16[128,512]{0,1:T(8,128)(2,1)S(1)}, bf16[128,512]{0,1:T(8,128)(2,1)S(1)}, u32[]{:S(2)}, u32[]{:S(2)}) collective-permute-start(bf16[128,512]{0,1:T(8,128)(2,1)S(1)} %get-tuple-element.782), channel_id=1, source_target_pairs={{0,2},{2,4},{4,6},{6,8},{8,10},{10,12},{12,14},{14,16},{16,18},{18... | collective-permute-start | bytes 393224 | tf_op jit(solution)/shard_map/while/body/eval_jaxpr/ppermute | solution.py:16
  260.4 12.3 %collective-permute-start.2 = (f32[128,512]{0,1:T(8,128)}, f32[128,512]{0,1:T(8,128)}, u32[]{:S(2)}, u32[]{:S(2)}) collective-permute-start(f32[128,512]{0,1:T(8,128)} %get-tuple-element.783), channel_id=1, source_target_pairs={{30,0},{0,2},{2,4},{4,6},{6,8},{8,10},{10,12},{12,14},{14,16},{16,... | collective-permute-start | bytes 786440 | tf_op jit(solution)/shard_map/while/body/eval_jaxpr/ppermute | solution.py:22
  274.4 7.2 %collective-permute-start.1 = (bf16[128,512]{0,1:T(8,128)(2,1)S(1)}, bf16[128,512]{0,1:T(8,128)(2,1)S(1)}, u32[]{:S(2)}, u32[]{:S(2)}) collective-permute-start(bf16[128,512]{0,1:T(8,128)(2,1)S(1)} %get-tuple-element.782), channel_id=1, source_target_pairs={{0,2},{2,4},{4,6},{6,8},{8,10},{10,12},{12,14},{14,16},{16,18},{18... | collective-permute-start | bytes 393224 | tf_op jit(solution)/shard_map/while/body/eval_jaxpr/ppermute | solution.py:16
  276.1 11.8 %collective-permute-start.2 = (f32[128,512]{0,1:T(8,128)}, f32[128,512]{0,1:T(8,128)}, u32[]{:S(2)}, u32[]{:S(2)}) collective-permute-start(f32[128,512]{0,1:T(8,128)} %get-tuple-element.783), channel_id=1, source_target_pairs={{30,0},{0,2},{2,4},{4,6},{6,8},{8,10},{10,12},{12,14},{14,16},{16,... | collective-permute-start | bytes 786440 | tf_op jit(solution)/shard_map/while/body/eval_jaxpr/ppermute | solution.py:22
  289.5 8.2 %collective-permute-start.1 = (bf16[128,512]{0,1:T(8,128)(2,1)S(1)}, bf16[128,512]{0,1:T(8,128)(2,1)S(1)}, u32[]{:S(2)}, u32[]{:S(2)}) collective-permute-start(bf16[128,512]{0,1:T(8,128)(2,1)S(1)} %get-tuple-element.782), channel_id=1, source_target_pairs={{0,2},{2,4},{4,6},{6,8},{8,10},{10,12},{12,14},{14,16},{16,18},{18... | collective-permute-start | bytes 393224 | tf_op jit(solution)/shard_map/while/body/eval_jaxpr/ppermute | solution.py:16
  291.9 11.3 %collective-permute-start.2 = (f32[128,512]{0,1:T(8,128)}, f32[128,512]{0,1:T(8,128)}, u32[]{:S(2)}, u32[]{:S(2)}) collective-permute-start(f32[128,512]{0,1:T(8,128)} %get-tuple-element.783), channel_id=1, source_target_pairs={{30,0},{0,2},{2,4},{4,6},{6,8},{8,10},{10,12},{12,14},{14,16},{16,... | collective-permute-start | bytes 786440 | tf_op jit(solution)/shard_map/while/body/eval_jaxpr/ppermute | solution.py:22
  305.0 8.6 %collective-permute-start.1 = (bf16[128,512]{0,1:T(8,128)(2,1)S(1)}, bf16[128,512]{0,1:T(8,128)(2,1)S(1)}, u32[]{:S(2)}, u32[]{:S(2)}) collective-permute-start(bf16[128,512]{0,1:T(8,128)(2,1)S(1)} %get-tuple-element.782), channel_id=1, source_target_pairs={{0,2},{2,4},{4,6},{6,8},{8,10},{10,12},{12,14},{14,16},{16,18},{18... | collective-permute-start | bytes 393224 | tf_op jit(solution)/shard_map/while/body/eval_jaxpr/ppermute | solution.py:16
  307.4 10.3 %collective-permute-start.2 = (f32[128,512]{0,1:T(8,128)}, f32[128,512]{0,1:T(8,128)}, u32[]{:S(2)}, u32[]{:S(2)}) collective-permute-start(f32[128,512]{0,1:T(8,128)} %get-tuple-element.783), channel_id=1, source_target_pairs={{30,0},{0,2},{2,4},{4,6},{6,8},{8,10},{10,12},{12,14},{14,16},{16,... | collective-permute-start | bytes 786440 | tf_op jit(solution)/shard_map/while/body/eval_jaxpr/ppermute | solution.py:22
  319.4 9.3 %collective-permute-start.1 = (bf16[128,512]{0,1:T(8,128)(2,1)S(1)}, bf16[128,512]{0,1:T(8,128)(2,1)S(1)}, u32[]{:S(2)}, u32[]{:S(2)}) collective-permute-start(bf16[128,512]{0,1:T(8,128)(2,1)S(1)} %get-tuple-element.782), channel_id=1, source_target_pairs={{0,2},{2,4},{4,6},{6,8},{8,10},{10,12},{12,14},{14,16},{16,18},{18... | collective-permute-start | bytes 393224 | tf_op jit(solution)/shard_map/while/body/eval_jaxpr/ppermute | solution.py:16
  323.2 10.4 %collective-permute-start.2 = (f32[128,512]{0,1:T(8,128)}, f32[128,512]{0,1:T(8,128)}, u32[]{:S(2)}, u32[]{:S(2)}) collective-permute-start(f32[128,512]{0,1:T(8,128)} %get-tuple-element.783), channel_id=1, source_target_pairs={{30,0},{0,2},{2,4},{4,6},{6,8},{8,10},{10,12},{12,14},{14,16},{16,... | collective-permute-start | bytes 786440 | tf_op jit(solution)/shard_map/while/body/eval_jaxpr/ppermute | solution.py:22
  336.3 6.8 %collective-permute-start.3 = (bf16[128,512]{0,1:T(8,128)(2,1)S(1)}, bf16[128,512]{0,1:T(8,128)(2,1)S(1)}, u32[]{:S(2)}, u32[]{:S(2)}) collective-permute-start(bf16[128,512]{0,1:T(8,128)(2,1)S(1)} %convert_element_type.51), channel_id=1, source_target_pairs={{14,0},{16,2},{18,4},{20,6},{22,8},{24,10},{26,12},{28,14},{30,16}... | collective-permute-start | bytes 393224 | tf_op jit(solution)/shard_map/ppermute | solution.py:22
Sparse Core Ops, SparseCore 0:
  9.6 11.7 all-gather.3
  24.1 61.8 all-gather.5
  88.8 59.3 all-gather.7
  349.0 180.6 reduce-scatter.1
where the time goes:
time: 541 us; the launch traced here: 539 us
  waiting for transfers between devices  346 us (64%)
  starting transfers between devices  95.5 us (18%)
  other arithmetic  37.5 us (7%)
  matrix products  18 us (3%)
  between operations  14 us (3%)
  loops' own time  9.98 us (2%)
  blocking collectives  9.29 us (2%)
  local copies, waits for them, and re-layouts  8.96 us (2%)
    reduce_scatter x1, waiting for transfers between devices, per_device(): lax.psum_scatter(lax.dot_general(features, gradients_lowered, (((0,), (0,...  167 us
    ppermute x14, starting transfers between devices, passed_along(): lax.ppermute(value, axis, [(source, source + steps) for source in range(l...  67.5 us
    all_gather x1, waiting for transfers between devices, per_device(): lax.all_gather(key_weight, 'cp', axis=0, tiled=True)  64.7 us
    all_gather x1, waiting for transfers between devices, per_device(): lax.all_gather(value_projection_weight, 'cp', axis=0, tiled=True)  59.8 us
    ppermute x8, waiting for transfers between devices, from_behind(): return lax.ppermute(block, axis, route)  40.1 us
    ppermute x8, starting transfers between devices, from_behind(): return lax.ppermute(block, axis, route)  27.9 us
    and x15, other arithmetic, visible(): (key_pos[None, :] >= doc_start[:, None]) & (key_pos[None, :] <= query_pos...  20.1 us
    add x14, other arithmetic, backward_turn(): return (kv_block, sums_now + pair_part, query_now + query_part)  13.3 us
  transfers between devices with their start and end apart: 26, of which 19 were waited for; matrix products, arithmetic and copies ran while one was open for 6% of the time, Pallas kernels for 0%

commit v1 on v0

--- a/solution.py
+++ b/solution.py
@@ -1,6 +1,10 @@
+import functools
+
 import jax
 import jax.numpy as jnp
 from jax import lax
+from jax.experimental import pallas as pl
+from jax.experimental.pallas import tpu as pltpu
 from jax.sharding import PartitionSpec as P
 
 HEAD_SIZE = 128
@@ -194,18 +198,471 @@
     )
 
 
+PLANE = 4
+
+
+def fused_fits(mesh, model_width, tokens):
+    cp, tp = mesh.shape["cp"], mesh.shape["tp"]
+    if cp % SPAN or cp % (PLANE * tp) or SPAN % PLANE or tp != 2:
+        return False
+    return model_width % (cp * HEAD_SIZE) == 0 and tokens // cp == HEAD_SIZE
+
+
+def exchange_kernel(
+    count_cp,
+    kv_heads,
+    q_per_kv,
+    hid,
+    qry,
+    gout,
+    wk,
+    wv,
+    starts,
+    dq_out,
+    gh_out,
+    gwk_out,
+    gwv_out,
+    xp,
+    wz,
+    wo,
+    part,
+    summed,
+    kvg,
+    qs,
+    gs,
+    s_scr,
+    dp_scr,
+    dqt,
+    dpart,
+    dsend,
+    drecv,
+    dkvp,
+    gwown,
+    gws,
+    gwr,
+    ghs,
+    gho,
+    x_send,
+    x_recv,
+    w_send,
+    w_recv,
+    o_send,
+    o_recv,
+    r_send,
+    r_recv,
+    k_send,
+    k_recv,
+    d_send,
+    d_recv,
+    p_send,
+    p_recv,
+    g_send,
+    g_recv,
+    h_send,
+    h_recv,
+):
+    tokens = hid.shape[0]
+    depth = wk.shape[0]
+    half = wk.shape[1]
+    cols = count_cp // PLANE
+    per_tp = cols // 2
+    stack = q_per_kv * tokens
+    inv_sqrt = HEAD_SIZE ** (-0.5)
+    f32 = jnp.float32
+    bf16 = jnp.bfloat16
+    c = lax.axis_index("cp")
+    t = lax.axis_index("tp")
+    ot = 1 - t
+    z = c // PLANE
+    p = c % PLANE
+    j = c % SPAN
+    base = c - j
+
+    def remote(src, dst, ss, rs, cp, tp):
+        return pltpu.make_async_remote_copy(
+            src_ref=src,
+            dst_ref=dst,
+            send_sem=ss,
+            recv_sem=rs,
+            device_id=(cp, tp),
+            device_id_type=pl.DeviceIdType.MESH,
+        )
+
+    def at_plane(pp):
+        return z * PLANE + pp
+
+    barrier = pltpu.get_barrier_semaphore()
+    greeted = 0
+
+    def greet(cp, tp):
+        pl.semaphore_signal(
+            barrier, inc=1, device_id=(cp, tp), device_id_type=pl.DeviceIdType.MESH
+        )
+
+    for d in range(1, SPAN):
+        greet(base + (j + d) % SPAN, t)
+        greeted += 1
+    for d in range(PLANE):
+        greet(at_plane((p + d) % PLANE), ot)
+        greeted += 1
+    planes = SPAN // PLANE
+    for d in range(cols - planes):
+        greet((((z // planes) * planes + planes + d) % cols) * PLANE + p, t)
+        greeted += 1
+    wz[z, :, :half] = wk[...]
+    wz[z, :, half:] = wv[...]
+    pl.semaphore_wait(barrier, greeted)
+
+    sends = []
+
+    for d in range(1, cols):
+        copy = remote(
+            wz.at[z],
+            wz.at[z],
+            w_send.at[d],
+            w_recv.at[z],
+            ((z + d) % cols) * PLANE + p,
+            t,
+        )
+        copy.start()
+        sends.append(copy)
+    for tt in range(2):
+        for d in range(PLANE):
+            if tt == 0 and d == 0:
+                continue
+            pp = (p + d) % PLANE
+            for k in range(per_tp):
+                lane = pl.multiple_of((k * PLANE + pp) * depth, HEAD_SIZE)
+                copy = remote(
+                    hid.at[:, pl.ds(lane, depth)],
+                    xp.at[t * per_tp + k, p],
+                    x_send.at[tt, d, k],
+                    x_recv.at[t, p, k],
+                    at_plane(pp),
+                    (t + tt) % 2,
+                )
+                copy.start()
+                sends.append(copy)
+    for k in range(per_tp):
+        lane = pl.multiple_of((k * PLANE + p) * depth, HEAD_SIZE)
+        xp[t * per_tp + k, p] = hid[:, pl.ds(lane, depth)]
+    for h in range(kv_heads * q_per_kv):
+        g, r = h // q_per_kv, h % q_per_kv
+        lanes = slice(h * HEAD_SIZE, (h + 1) * HEAD_SIZE)
+        qs[g, r * tokens : (r + 1) * tokens] = qry[:, lanes]
+        gs[g, r * tokens : (r + 1) * tokens] = gout[:, lanes]
+
+    for tt in range(2):
+        for d in range(PLANE):
+            if tt == 0 and d == 0:
+                continue
+            src_t, src_p = (t + tt) % 2, (p + d) % PLANE
+            for k in range(per_tp):
+                slot = xp.at[src_t * per_tp + k, src_p]
+                remote(
+                    slot, slot, x_send.at[tt, d, k], x_recv.at[src_t, src_p, k], at_plane(src_p), src_t if tt else t
+                ).wait_recv()
+
+    def project(zz, first):
+        lhs = xp[zz].reshape(PLANE * tokens, depth)
+        add = jnp.dot(lhs, wz[zz], preferred_element_type=f32).reshape(part.shape)
+        if first:
+            part[...] = add
+        else:
+            part[...] += add
+
+    project(z, True)
+    for d in range(1, cols):
+        zz = (z + d) % cols
+        remote(wz.at[zz], wz.at[zz], w_send.at[d], w_recv.at[zz], zz * PLANE + p, t).wait_recv()
+        project(zz, False)
+    for d in range(1, PLANE):
+        pp = (p + d) % PLANE
+        copy = remote(part.at[pp], summed.at[p], r_send.at[d], r_recv.at[p], at_plane(pp), t)
+        copy.start()
+        sends.append(copy)
+    for k in range(per_tp):
+        copy = remote(wz.at[ot * per_tp + k], wo.at[k], o_send.at[k], o_recv.at[k], c, ot)
+        copy.start()
+        sends.append(copy)
+    total = part[p]
+    for d in range(1, PLANE):
+        pp = (p + d) % PLANE
+        remote(
+            summed.at[pp], summed.at[pp], r_send.at[d], r_recv.at[pp], at_plane(pp), t
+        ).wait_recv()
+        total = total + summed[pp]
+    kvg[j] = total.astype(bf16)
+
+    def kv_copy(d):
+        return remote(kvg.at[j], kvg.at[j], k_send.at[d], k_recv.at[j], c + d, t)
+
+    for d in range(1, SPAN):
+
+        @pl.when(j + d < SPAN)
+        def _():
+            kv_copy(d).start()
+
+    for d in range(1, SPAN):
+
+        @pl.when(j >= d)
+        def _():
+            slot = kvg.at[j - d]
+            remote(slot, slot, k_send.at[d], k_recv.at[j - d], c - d, t).wait_recv()
+
+    row = lax.broadcasted_iota(jnp.int32, (tokens, tokens), 0)
+    lane = lax.broadcasted_iota(jnp.int32, (tokens, tokens), 1)
+    start_row = starts[...]
+
+    def fold(value, op):
+        return op(value.reshape(tokens // 8, 8, stack), axis=0)
+
+    nt = (((1,), (1,)), ((), ()))
+    tn = (((0,), (0,)), ((), ()))
+    for g in range(kv_heads):
+        kcol = slice(g * HEAD_SIZE, (g + 1) * HEAD_SIZE)
+        vcol = slice(half + g * HEAD_SIZE, half + (g + 1) * HEAD_SIZE)
+
+        def first_pass(i, top):
+            key_pos = (base + i) * tokens + row
+            seen = (key_pos >= start_row) & (key_pos <= c * tokens + lane)
+            bias = jnp.where(seen, 0.0, NEG_FILL)
+            bias = jnp.concatenate([bias] * q_per_kv, axis=1)
+            s = lax.dot_general(kvg[i, :, kcol], qs[g], nt, preferred_element_type=f32)
+            s = s * inv_sqrt + bias
+            s_scr[i] = s
+            dp_scr[i] = lax.dot_general(kvg[i, :, vcol], gs[g], nt, preferred_element_type=f32)
+            return jnp.maximum(top, fold(s, jnp.max))
+
+        top = lax.fori_loop(0, j + 1, first_pass, jnp.full((8, stack), NEG_FILL, f32))
+        top = jnp.max(top, axis=0, keepdims=True)
+
+        def second_pass(i, carried):
+            count, dot = carried
+            e = jnp.exp(s_scr[i] - top)
+            s_scr[i] = e
+            return count + fold(e, jnp.sum), dot + fold(e * dp_scr[i], jnp.sum)
+
+        zero = jnp.zeros((8, stack), f32)
+        count, dot = lax.fori_loop(0, j + 1, second_pass, (zero, zero))
+        inv_count = 1.0 / jnp.sum(count, axis=0, keepdims=True)
+        delta = jnp.sum(dot, axis=0, keepdims=True) * inv_count
+        dqt[...] = jnp.zeros_like(dqt)
+
+        def third_pass(i, carried):
+            probs = s_scr[i] * inv_count
+            ds = (probs * (dp_scr[i] - delta)).astype(bf16)
+            dpart[i, :, vcol] = jnp.dot(probs.astype(bf16), gs[g], preferred_element_type=f32)
+            dpart[i, :, kcol] = jnp.dot(ds, qs[g], preferred_element_type=f32) * inv_sqrt
+            dqt[...] += lax.dot_general(kvg[i, :, kcol], ds, tn, preferred_element_type=f32)
+            return carried
+
+        lax.fori_loop(0, j + 1, third_pass, 0)
+        for r in range(q_per_kv):
+            h = g * q_per_kv + r
+            tile = dqt[:, r * tokens : (r + 1) * tokens]
+            dq_out[:, h * HEAD_SIZE : (h + 1) * HEAD_SIZE] = (tile.T * inv_sqrt).astype(bf16)
+
+    def grad_copy(d):
+        return remote(dsend.at[d], drecv.at[d], d_send.at[d], d_recv.at[d], c - d, t)
+
+    for d in range(1, SPAN):
+
+        @pl.when(j >= d)
+        def _():
+            dsend[d] = dpart[j - d].astype(bf16)
+            grad_copy(d).start()
+
+    dpart[0] = dpart[j]
+    for d in range(1, SPAN):
+
+        @pl.when(j + d < SPAN)
+        def _():
+            slot = drecv.at[d]
+            remote(slot, slot, d_send.at[d], d_recv.at[d], c + d, t).wait_recv()
+            dpart[0] += drecv[d].astype(f32)
+
+    dkvp[t, p] = dpart[0].astype(bf16)
+    for tt in range(2):
+        for d in range(PLANE):
+            if tt == 0 and d == 0:
+                continue
+            copy = remote(
+                dkvp.at[t, p],
+                dkvp.at[t, p],
+                p_send.at[tt, d],
+                p_recv.at[t, p],
+                at_plane((p + d) % PLANE),
+                (t + tt) % 2,
+            )
+            copy.start()
+            sends.append(copy)
+
+    def wait_plane(tt):
+        for d in range(1 - tt, PLANE):
+            src_t, src_p = (t + tt) % 2, (p + d) % PLANE
+            slot = dkvp.at[src_t, src_p]
+            remote(
+                slot, slot, p_send.at[tt, d], p_recv.at[src_t, src_p], at_plane(src_p), src_t
+            ).wait_recv()
+
+    wait_plane(0)
+    mine = dkvp[t].reshape(PLANE * tokens, 2 * half)
+
+    def weight_part(zz):
+        lhs = xp[zz].reshape(PLANE * tokens, depth)
+        return lax.dot_general(lhs, mine, tn, preferred_element_type=f32)
+
+    for d in range(1, cols):
+        gws[d] = weight_part((z + d) % cols).astype(bf16)
+        copy = remote(
+            gws.at[d],
+            gwr.at[d],
+            g_send.at[d],
+            g_recv.at[d],
+            ((z + d) % cols) * PLANE + p,
+            t,
+        )
+        copy.start()
+        sends.append(copy)
+    wait_plane(1)
+    for k in range(per_tp):
+        remote(wo.at[k], wo.at[k], o_send.at[k], o_recv.at[k], c, ot).wait_recv()
+    other = dkvp[ot].reshape(PLANE * tokens, 2 * half)
+    for k in range(per_tp):
+        value = lax.dot_general(mine, wz[t * per_tp + k], nt, preferred_element_type=f32)
+        value = value + lax.dot_general(other, wo[k], nt, preferred_element_type=f32)
+        ghs[:, k] = value.astype(bf16).reshape(PLANE, tokens, depth)
+    for tt in range(2):
+        for d in range(PLANE):
+            if tt == 0 and d == 0:
+                continue
+            pp = (p + d) % PLANE
+            copy = remote(
+                ghs.at[pp],
+                gho.at[p, t],
+                h_send.at[tt, d],
+                h_recv.at[p, t],
+                at_plane(pp),
+                (t + tt) % 2,
+            )
+            copy.start()
+            sends.append(copy)
+    gho[p, t] = ghs[p]
+    gwown[...] = weight_part(z)
+    for tt in range(2):
+        for d in range(PLANE):
+            if tt == 0 and d == 0:
+                continue
+            src_t, src_p = (t + tt) % 2, (p + d) % PLANE
+            slot = gho.at[src_p, src_t]
+            remote(
+                slot, slot, h_send.at[tt, d], h_recv.at[src_p, src_t], at_plane(src_p), src_t
+            ).wait_recv()
+    for zz in range(cols):
+        for pp in range(PLANE):
+            block = (zz * PLANE + pp) * depth
+            gh_out[:, block : block + depth] = gho[pp, zz // per_tp, zz % per_tp]
+    total = gwown[...]
+    for d in range(1, cols):
+        slot = gwr.at[d]
+        remote(slot, slot, g_send.at[d], g_recv.at[d], ((z + d) % cols) * PLANE + p, t).wait_recv()
+        total = total + gwr[d].astype(f32)
+    gwk_out[...] = total[:, :half]
+    gwv_out[...] = total[:, half:]
+    for copy in sends:
+        copy.wait_send()
+    for d in range(1, SPAN):
+
+        @pl.when(j + d < SPAN)
+        def _():
+            kv_copy(d).wait_send()
+
+        @pl.when(j >= d)
+        def _():
+            grad_copy(d).wait_send()
+
+
+def fused_device(hidden_states, query, attention_output_gradient, key_weight, value_weight, doc_start):
+    tokens, width = hidden_states.shape
+    depth, half = key_weight.shape
+    count_cp = lax.axis_size("cp")
+    cols = count_cp // PLANE
+    per_tp = cols // 2
+    kv_heads = half // HEAD_SIZE
+    q_per_kv = query.shape[1] // half
+    stack = q_per_kv * tokens
+    pair = 2 * half
+    bf16, f32 = jnp.bfloat16, jnp.float32
+    starts = jnp.broadcast_to(doc_start[None, :], (8, tokens))[:1]
+    dma = pltpu.SemaphoreType.DMA
+    vmem = pltpu.VMEM
+    spec = pl.BlockSpec(memory_space=pltpu.VMEM)
+    return pl.pallas_call(
+        functools.partial(exchange_kernel, count_cp, kv_heads, q_per_kv),
+        out_shape=(
+            jax.ShapeDtypeStruct(query.shape, bf16),
+            jax.ShapeDtypeStruct((tokens, 2 * width), bf16),
+            jax.ShapeDtypeStruct((depth, half), f32),
+            jax.ShapeDtypeStruct((depth, half), f32),
+        ),
+        in_specs=[spec] * 6,
+        out_specs=(spec,) * 4,
+        scratch_shapes=[
+            vmem((cols, PLANE, tokens, depth), bf16),
+            vmem((cols, depth, pair), bf16),
+            vmem((per_tp, depth, pair), bf16),
+            vmem((PLANE, tokens, pair), f32),
+            vmem((PLANE, tokens, pair), f32),
+            vmem((SPAN, tokens, pair), bf16),
+            vmem((kv_heads, stack, HEAD_SIZE), bf16),
+            vmem((kv_heads, stack, HEAD_SIZE), bf16),
+            vmem((SPAN, tokens, stack), f32),
+            vmem((SPAN, tokens, stack), f32),
+            vmem((HEAD_SIZE, stack), f32),
+            vmem((SPAN, tokens, pair), f32),
+            vmem((SPAN, tokens, pair), bf16),
+            vmem((SPAN, tokens, pair), bf16),
+            vmem((2, PLANE, tokens, pair), bf16),
+            vmem((depth, pair), f32),
+            vmem((cols, depth, pair), bf16),
+            vmem((cols, depth, pair), bf16),
+            vmem((PLANE, per_tp, tokens, depth), bf16),
+            vmem((PLANE, 2, per_tp, tokens, depth), bf16),
+            dma((2, PLANE, per_tp)),
+            dma((2, PLANE, per_tp)),
+            dma((cols,)),
+            dma((cols,)),
+            dma((per_tp,)),
+            dma((per_tp,)),
+            dma((PLANE,)),
+            dma((PLANE,)),
+            dma((SPAN,)),
+            dma((SPAN,)),
+            dma((SPAN,)),
+            dma((SPAN,)),
+            dma((2, PLANE)),
+            dma((2, PLANE)),
+            dma((cols,)),
+            dma((cols,)),
+            dma((2, PLANE)),
+            dma((PLANE, 2)),
+        ],
+        compiler_params=pltpu.CompilerParams(
+            collective_id=0, has_side_effects=True, vmem_limit_bytes=56 * 1024 * 1024
+        ),
+    )(hidden_states, query, attention_output_gradient, key_weight, value_weight, starts)
+
+
 def solution(mesh):
-    return jax.shard_map(
-        per_device,
-        mesh=mesh,
-        in_specs=(
-            P("cp", "tp"),
-            P("cp", "tp"),
-            P("cp", "tp"),
-            P("cp", "tp"),
-            P("cp", "tp"),
-            P("cp"),
-        ),
-        out_specs=(P("cp", "tp"), P("cp", None), P("cp", "tp"), P("cp", "tp")),
-        check_vma=False,
-    )
+    def run(*arrays):
+        fits = fused_fits(mesh, arrays[0].shape[1], arrays[0].shape[0])
+        return jax.shard_map(
+            fused_device if fits else per_device,
+            mesh=mesh,
+            in_specs=(P("cp", "tp"),) * 5 + (P("cp"),),
+            out_specs=(P("cp", "tp"), P("cp", None), P("cp", "tp"), P("cp", "tp")),
+            check_vma=False,
+        )(*arrays)
+
+    return run

time: 541 us -> 116 us (0.21)
  waiting for transfers between devices: 346 us -> 0 us
  Pallas kernels: 0 us -> 110 us
  starting transfers between devices: 95.5 us -> 0 us
  other arithmetic: 37.5 us -> 0 us
  matrix products: 18 us -> 0 us
  between operations: 14 us -> 0.65 us
  loops' own time: 9.98 us -> 0 us
  blocking collectives: 9.29 us -> 0 us
    reduce_scatter x1 -> x0, waiting for transfers between devices: 167 us -> none  [per_device(): lax.psum_scatter(lax.dot_general(features, gradients_lowered, (((0,), (0,...]
    all_gather x3 -> x0, waiting for transfers between devices: 134 us -> none  [the longest x1 64.7 us: per_device(): lax.all_gather(key_weight, 'cp', axis=0, tiled=True)]
    pallas_call x0 -> x1, Pallas kernels: none -> 110 us  [fused_device(): pl.pallas_call(functools.partial(exchange_kernel, count_cp, kv_heads, q_p...]
    ppermute x22 -> x0, starting transfers between devices: 95.4 us -> none  [the longest x14 67.5 us: passed_along(): lax.ppermute(value, axis, [(source, source + steps) for source in range(l...]
    ppermute x22 -> x0, waiting for transfers between devices: 43.2 us -> none  [the longest x8 40.1 us: from_behind(): return lax.ppermute(block, axis, route)]
    and x15 -> x0, other arithmetic: 20.1 us -> none  [visible(): (key_pos[None, :] >= doc_start[:, None]) & (key_pos[None, :] <= query_pos...]
    dot_general x10 -> x0, matrix products: 18 us -> none  [the longest x1 5.68 us: per_device(): lax.dot_general(features, gradients_lowered, (((0,), (0,)), ((), ())), pr...]
    add x44 -> x0, other arithmetic: 14 us -> none  [the longest x14 13.3 us: backward_turn(): return (kv_block, sums_now + pair_part, query_now + query_part)]
  transfers between devices with their start and end apart: 26 -> 0, of which waited for: 19 -> 0; matrix products, arithmetic and copies ran while one was open for 6% -> 0% of each run, Pallas kernels for 0% -> 0%
where the time goes in v1:
time: 116 us; the launch traced here: 115 us
  Pallas kernels  110 us (95%)
  local copies, waits for them, and re-layouts  4.81 us (4%)
    pallas_call x1, Pallas kernels, fused_device(): pl.pallas_call(functools.partial(exchange_kernel, count_cp, kv_heads, q_p...  110 us
    unnamed x10, local copies, waits for them, and re-layouts  4.81 us

profile of v1, /device:TPU:0, one launch (start us, length us, event | category | flops | bytes accessed | tf_op | source)
XLA Modules:
  0.0 115.5 jit_solution(14811754658913826412)
XLA Ops:
  0.6 110.0 %shard_map.93 = (bf16[128,2048]{1,0:T(8,128)(2,1)}, bf16[128,4096]{1,0:T(8,128)(2,1)}, f32[256,256]{1,0:T(8,128)}, f32[256,256]{1,0:T(8,128)}) custom-call(bf16[128,2048]{1,0:T(8,128)(2,1)} %hid.1, bf16[128,2048]{1,0:T(8,128)(2,1)} %qry.1, bf16[128,2048]{1,0:T(8,128)(2,1)} %gout.1, bf16[256,256]{1,0:T(8,128)(2,1)} %wk.1, bf16[256,256]{1,0:T(8,128)(2,1)} %wv.1, ...), custom_call_target="tpu_custom_call" | custom-call | tf_op jit(solution)/shard_map/pallas_call | solution.py:601
  110.6 0.0 copy-start
  110.6 2.0 %copy.14 = bf16[128,2048]{1,0:T(8,128)(2,1)} copy(bf16[128,2048]{1,0:T(8,128)(2,1)} %get-tuple-element.8) | data formatting | bytes 1048576
  112.6 0.0 copy-done
  112.6 0.0 copy-start.2
  112.6 1.0 copy.15
  113.6 0.1 copy-done.2
  113.7 0.0 copy-start.1
  113.7 0.7 copy.16
  114.4 0.3 copy-done.1
  114.8 0.7 copy.17
Async XLA Ops:
  110.6 2.0 %copy-start = (bf16[128,4096]{1,0:T(8,128)(2,1)S(1)}, bf16[128,4096]{1,0:T(8,128)(2,1)}, u32[]{:S(2)}) copy-start(bf16[128,4096]{1,0:T(8,128)(2,1)} %get-tuple-element.9) | copy-start | bytes 3145732
  112.6 1.1 copy-start.2
  113.7 1.0 copy-start.1

commit v2 on v1

--- a/solution.py
+++ b/solution.py
@@ -263,7 +263,7 @@
 ):
     tokens = hid.shape[0]
     depth = wk.shape[0]
-    half = wk.shape[1]
+    pair = 2 * HEAD_SIZE
     cols = count_cp // PLANE
     per_tp = cols // 2
     stack = q_per_kv * tokens
@@ -309,40 +309,44 @@
     for d in range(cols - planes):
         greet((((z // planes) * planes + planes + d) % cols) * PLANE + p, t)
         greeted += 1
-    wz[z, :, :half] = wk[...]
-    wz[z, :, half:] = wv[...]
+    for g in range(kv_heads):
+        lanes = slice(g * HEAD_SIZE, (g + 1) * HEAD_SIZE)
+        wz[g, z, :, :HEAD_SIZE] = wk[:, lanes]
+        wz[g, z, :, HEAD_SIZE:] = wv[:, lanes]
     pl.semaphore_wait(barrier, greeted)
 
     sends = []
 
-    for d in range(1, cols):
-        copy = remote(
-            wz.at[z],
-            wz.at[z],
-            w_send.at[d],
-            w_recv.at[z],
-            ((z + d) % cols) * PLANE + p,
-            t,
-        )
-        copy.start()
-        sends.append(copy)
-    for tt in range(2):
-        for d in range(PLANE):
-            if tt == 0 and d == 0:
-                continue
-            pp = (p + d) % PLANE
-            for k in range(per_tp):
-                lane = pl.multiple_of((k * PLANE + pp) * depth, HEAD_SIZE)
-                copy = remote(
-                    hid.at[:, pl.ds(lane, depth)],
-                    xp.at[t * per_tp + k, p],
-                    x_send.at[tt, d, k],
-                    x_recv.at[t, p, k],
-                    at_plane(pp),
-                    (t + tt) % 2,
-                )
-                copy.start()
-                sends.append(copy)
+    def column(d):
+        return ((z + d) % cols) * PLANE + p
+
+    def plane_peers():
+        return [(tt, d) for tt in range(2) for d in range(PLANE) if tt or d]
+
+    def send_weights(g):
+        for d in range(1, cols):
+            slot = wz.at[g, z]
+            copy = remote(slot, slot, w_send.at[g, d], w_recv.at[g, z], column(d), t)
+            copy.start()
+            sends.append(copy)
+
+    send_weights(0)
+    for tt, d in plane_peers():
+        pp = (p + d) % PLANE
+        for k in range(per_tp):
+            lane = pl.multiple_of((k * PLANE + pp) * depth, HEAD_SIZE)
+            copy = remote(
+                hid.at[:, pl.ds(lane, depth)],
+                xp.at[t * per_tp + k, p],
+                x_send.at[tt, d, k],
+                x_recv.at[t, p, k],
+                at_plane(pp),
+                (t + tt) % 2,
+            )
+            copy.start()
+            sends.append(copy)
+    for g in range(1, kv_heads):
+        send_weights(g)
     for k in range(per_tp):
         lane = pl.multiple_of((k * PLANE + p) * depth, HEAD_SIZE)
         xp[t * per_tp + k, p] = hid[:, pl.ds(lane, depth)]
@@ -352,66 +356,61 @@
         qs[g, r * tokens : (r + 1) * tokens] = qry[:, lanes]
         gs[g, r * tokens : (r + 1) * tokens] = gout[:, lanes]
 
-    for tt in range(2):
-        for d in range(PLANE):
-            if tt == 0 and d == 0:
-                continue
-            src_t, src_p = (t + tt) % 2, (p + d) % PLANE
-            for k in range(per_tp):
-                slot = xp.at[src_t * per_tp + k, src_p]
-                remote(
-                    slot, slot, x_send.at[tt, d, k], x_recv.at[src_t, src_p, k], at_plane(src_p), src_t if tt else t
-                ).wait_recv()
-
-    def project(zz, first):
-        lhs = xp[zz].reshape(PLANE * tokens, depth)
-        add = jnp.dot(lhs, wz[zz], preferred_element_type=f32).reshape(part.shape)
-        if first:
-            part[...] = add
-        else:
-            part[...] += add
-
-    project(z, True)
-    for d in range(1, cols):
-        zz = (z + d) % cols
-        remote(wz.at[zz], wz.at[zz], w_send.at[d], w_recv.at[zz], zz * PLANE + p, t).wait_recv()
-        project(zz, False)
-    for d in range(1, PLANE):
-        pp = (p + d) % PLANE
-        copy = remote(part.at[pp], summed.at[p], r_send.at[d], r_recv.at[p], at_plane(pp), t)
-        copy.start()
-        sends.append(copy)
-    for k in range(per_tp):
-        copy = remote(wz.at[ot * per_tp + k], wo.at[k], o_send.at[k], o_recv.at[k], c, ot)
-        copy.start()
-        sends.append(copy)
-    total = part[p]
-    for d in range(1, PLANE):
-        pp = (p + d) % PLANE
-        remote(
-            summed.at[pp], summed.at[pp], r_send.at[d], r_recv.at[pp], at_plane(pp), t
-        ).wait_recv()
-        total = total + summed[pp]
-    kvg[j] = total.astype(bf16)
-
-    def kv_copy(d):
-        return remote(kvg.at[j], kvg.at[j], k_send.at[d], k_recv.at[j], c + d, t)
-
-    for d in range(1, SPAN):
-
-        @pl.when(j + d < SPAN)
-        def _():
-            kv_copy(d).start()
-
-    for d in range(1, SPAN):
-
-        @pl.when(j >= d)
-        def _():
-            slot = kvg.at[j - d]
-            remote(slot, slot, k_send.at[d], k_recv.at[j - d], c - d, t).wait_recv()
+    for tt, d in plane_peers():
+        src_t, src_p = (t + tt) % 2, (p + d) % PLANE
+        for k in range(per_tp):
+            slot = xp.at[src_t * per_tp + k, src_p]
+            remote(
+                slot, slot, x_send.at[tt, d, k], x_recv.at[src_t, src_p, k], at_plane(src_p), src_t
+            ).wait_recv()
+
+    def project(g):
+        for d in range(cols):
+            zz = (z + d) % cols
+            slot = wz.at[g, zz]
+            if d:
+                remote(slot, slot, w_send.at[g, d], w_recv.at[g, zz], column(d), t).wait_recv()
+            lhs = xp[zz].reshape(PLANE * tokens, depth)
+            add = jnp.dot(lhs, wz[g, zz], preferred_element_type=f32)
+            add = add.reshape(PLANE, tokens, pair)
+            if d:
+                part[g] += add
+            else:
+                part[g] = add
+        for d in range(1, PLANE):
+            pp = (p + d) % PLANE
+            copy = remote(
+                part.at[g, pp], summed.at[g, p], r_send.at[g, d], r_recv.at[g, p], at_plane(pp), t
+            )
+            copy.start()
+            sends.append(copy)
+        for k in range(per_tp):
+            copy = remote(
+                wz.at[g, ot * per_tp + k], wo.at[g, k], o_send.at[g, k], o_recv.at[g, k], c, ot
+            )
+            copy.start()
+            sends.append(copy)
+
+    def kv_copy(g, d):
+        slot = kvg.at[g, j]
+        return remote(slot, slot, k_send.at[g, d], k_recv.at[g, j], c + d, t)
+
+    def finish_keys(g):
+        total = part[g, p]
+        for d in range(1, PLANE):
+            pp = (p + d) % PLANE
+            slot = summed.at[g, pp]
+            remote(slot, slot, r_send.at[g, d], r_recv.at[g, pp], at_plane(pp), t).wait_recv()
+            total = total + summed[g, pp]
+        kvg[g, j] = total.astype(bf16)
+        for d in range(1, SPAN):
+
+            @pl.when(j + d < SPAN)
+            def _():
+                kv_copy(g, d).start()
 
     row = lax.broadcasted_iota(jnp.int32, (tokens, tokens), 0)
-    lane = lax.broadcasted_iota(jnp.int32, (tokens, tokens), 1)
+    lane_index = lax.broadcasted_iota(jnp.int32, (tokens, tokens), 1)
     start_row = starts[...]
 
     def fold(value, op):
@@ -419,23 +418,38 @@
 
     nt = (((1,), (1,)), ((), ()))
     tn = (((0,), (0,)), ((), ()))
-    for g in range(kv_heads):
-        kcol = slice(g * HEAD_SIZE, (g + 1) * HEAD_SIZE)
-        vcol = slice(half + g * HEAD_SIZE, half + (g + 1) * HEAD_SIZE)
-
-        def first_pass(i, top):
+    kcol = slice(0, HEAD_SIZE)
+    vcol = slice(HEAD_SIZE, 2 * HEAD_SIZE)
+
+    def grad_copy(g, d):
+        return remote(
+            dsend.at[g, d], drecv.at[g, d], d_send.at[g, d], d_recv.at[g, d], c - d, t
+        )
+
+    def attend(g, after_first, after_second):
+        def first_pass(d, top):
+            i = j - d
+
+            @pl.when(d > 0)
+            def _():
+                slot = kvg.at[g, i]
+                remote(slot, slot, k_send.at[g, 1], k_recv.at[g, i], c - d, t).wait_recv()
+
             key_pos = (base + i) * tokens + row
-            seen = (key_pos >= start_row) & (key_pos <= c * tokens + lane)
+            seen = (key_pos >= start_row) & (key_pos <= c * tokens + lane_index)
             bias = jnp.where(seen, 0.0, NEG_FILL)
             bias = jnp.concatenate([bias] * q_per_kv, axis=1)
-            s = lax.dot_general(kvg[i, :, kcol], qs[g], nt, preferred_element_type=f32)
+            s = lax.dot_general(kvg[g, i, :, kcol], qs[g], nt, preferred_element_type=f32)
             s = s * inv_sqrt + bias
             s_scr[i] = s
-            dp_scr[i] = lax.dot_general(kvg[i, :, vcol], gs[g], nt, preferred_element_type=f32)
+            dp_scr[i] = lax.dot_general(
+                kvg[g, i, :, vcol], gs[g], nt, preferred_element_type=f32
+            )
             return jnp.maximum(top, fold(s, jnp.max))
 
         top = lax.fori_loop(0, j + 1, first_pass, jnp.full((8, stack), NEG_FILL, f32))
         top = jnp.max(top, axis=0, keepdims=True)
+        after_first()
 
         def second_pass(i, carried):
             count, dot = carried
@@ -447,140 +461,154 @@
         count, dot = lax.fori_loop(0, j + 1, second_pass, (zero, zero))
         inv_count = 1.0 / jnp.sum(count, axis=0, keepdims=True)
         delta = jnp.sum(dot, axis=0, keepdims=True) * inv_count
+        after_second()
         dqt[...] = jnp.zeros_like(dqt)
 
         def third_pass(i, carried):
             probs = s_scr[i] * inv_count
             ds = (probs * (dp_scr[i] - delta)).astype(bf16)
-            dpart[i, :, vcol] = jnp.dot(probs.astype(bf16), gs[g], preferred_element_type=f32)
-            dpart[i, :, kcol] = jnp.dot(ds, qs[g], preferred_element_type=f32) * inv_sqrt
-            dqt[...] += lax.dot_general(kvg[i, :, kcol], ds, tn, preferred_element_type=f32)
+            dpart[g, i, :, vcol] = jnp.dot(probs.astype(bf16), gs[g], preferred_element_type=f32)
+            dpart[g, i, :, kcol] = jnp.dot(ds, qs[g], preferred_element_type=f32) * inv_sqrt
+            dqt[...] += lax.dot_general(kvg[g, i, :, kcol], ds, tn, preferred_element_type=f32)
             return carried
 
         lax.fori_loop(0, j + 1, third_pass, 0)
+        for d in range(1, SPAN):
+
+            @pl.when(j >= d)
+            def _():
+                dsend[g, d] = dpart[g, j - d].astype(bf16)
+                grad_copy(g, d).start()
+
         for r in range(q_per_kv):
             h = g * q_per_kv + r
             tile = dqt[:, r * tokens : (r + 1) * tokens]
             dq_out[:, h * HEAD_SIZE : (h + 1) * HEAD_SIZE] = (tile.T * inv_sqrt).astype(bf16)
 
-    def grad_copy(d):
-        return remote(dsend.at[d], drecv.at[d], d_send.at[d], d_recv.at[d], c - d, t)
-
-    for d in range(1, SPAN):
-
-        @pl.when(j >= d)
-        def _():
-            dsend[d] = dpart[j - d].astype(bf16)
-            grad_copy(d).start()
-
-    dpart[0] = dpart[j]
-    for d in range(1, SPAN):
-
-        @pl.when(j + d < SPAN)
-        def _():
-            slot = drecv.at[d]
-            remote(slot, slot, d_send.at[d], d_recv.at[d], c + d, t).wait_recv()
-            dpart[0] += drecv[d].astype(f32)
-
-    dkvp[t, p] = dpart[0].astype(bf16)
-    for tt in range(2):
-        for d in range(PLANE):
-            if tt == 0 and d == 0:
-                continue
+    def collect(g):
+        dpart[g, 0] = dpart[g, j]
+        for d in range(1, SPAN):
+
+            @pl.when(j + d < SPAN)
+            def _():
+                slot = drecv.at[g, d]
+                remote(slot, slot, d_send.at[g, d], d_recv.at[g, d], c + d, t).wait_recv()
+                dpart[g, 0] += drecv[g, d].astype(f32)
+
+        dkvp[t, g, p] = dpart[g, 0].astype(bf16)
+        for tt, d in plane_peers():
+            slot = dkvp.at[t, g, p]
             copy = remote(
-                dkvp.at[t, p],
-                dkvp.at[t, p],
-                p_send.at[tt, d],
-                p_recv.at[t, p],
+                slot,
+                slot,
+                p_send.at[g, tt, d],
+                p_recv.at[t, g, p],
                 at_plane((p + d) % PLANE),
                 (t + tt) % 2,
             )
             copy.start()
             sends.append(copy)
 
-    def wait_plane(tt):
+    def wait_plane(g, tt):
         for d in range(1 - tt, PLANE):
             src_t, src_p = (t + tt) % 2, (p + d) % PLANE
-            slot = dkvp.at[src_t, src_p]
+            slot = dkvp.at[src_t, g, src_p]
             remote(
-                slot, slot, p_send.at[tt, d], p_recv.at[src_t, src_p], at_plane(src_p), src_t
+                slot, slot, p_send.at[g, tt, d], p_recv.at[src_t, g, src_p], at_plane(src_p), src_t
             ).wait_recv()
 
-    wait_plane(0)
-    mine = dkvp[t].reshape(PLANE * tokens, 2 * half)
-
-    def weight_part(zz):
+    def plane_grads(tt, g):
+        return dkvp[tt, g].reshape(PLANE * tokens, pair)
+
+    def weight_part(g, zz):
         lhs = xp[zz].reshape(PLANE * tokens, depth)
-        return lax.dot_general(lhs, mine, tn, preferred_element_type=f32)
-
-    for d in range(1, cols):
-        gws[d] = weight_part((z + d) % cols).astype(bf16)
+        return lax.dot_general(lhs, plane_grads(t, g), tn, preferred_element_type=f32)
+
+    def send_weight_grads(g):
+        for d in range(1, cols):
+            gws[g, d] = weight_part(g, (z + d) % cols).astype(bf16)
+            copy = remote(
+                gws.at[g, d], gwr.at[g, d], g_send.at[g, d], g_recv.at[g, d], column(d), t
+            )
+            copy.start()
+            sends.append(copy)
+
+    def nothing():
+        pass
+
+    last = kv_heads - 1
+    project(0)
+    finish_keys(0)
+    for g in range(kv_heads):
+        if g < last:
+            project(g + 1)
+        attend(
+            g,
+            functools.partial(finish_keys, g + 1) if g < last else nothing,
+            functools.partial(collect, g - 1) if g else nothing,
+        )
+        if g:
+            wait_plane(g - 1, 0)
+            send_weight_grads(g - 1)
+    collect(last)
+    wait_plane(last, 0)
+    send_weight_grads(last)
+    for g in range(kv_heads):
+        wait_plane(g, 1)
+        for k in range(per_tp):
+            slot = wo.at[g, k]
+            remote(slot, slot, o_send.at[g, k], o_recv.at[g, k], c, ot).wait_recv()
+    for k in range(per_tp):
+        value = jnp.zeros((PLANE * tokens, depth), f32)
+        for g in range(kv_heads):
+            value += lax.dot_general(
+                plane_grads(t, g), wz[g, t * per_tp + k], nt, preferred_element_type=f32
+            )
+            value += lax.dot_general(
+                plane_grads(ot, g), wo[g, k], nt, preferred_element_type=f32
+            )
+        ghs[:, k] = value.astype(bf16).reshape(PLANE, tokens, depth)
+    for tt, d in plane_peers():
+        pp = (p + d) % PLANE
         copy = remote(
-            gws.at[d],
-            gwr.at[d],
-            g_send.at[d],
-            g_recv.at[d],
-            ((z + d) % cols) * PLANE + p,
-            t,
+            ghs.at[pp], gho.at[p, t], h_send.at[tt, d], h_recv.at[p, t], at_plane(pp), (t + tt) % 2
         )
         copy.start()
         sends.append(copy)
-    wait_plane(1)
-    for k in range(per_tp):
-        remote(wo.at[k], wo.at[k], o_send.at[k], o_recv.at[k], c, ot).wait_recv()
-    other = dkvp[ot].reshape(PLANE * tokens, 2 * half)
-    for k in range(per_tp):
-        value = lax.dot_general(mine, wz[t * per_tp + k], nt, preferred_element_type=f32)
-        value = value + lax.dot_general(other, wo[k], nt, preferred_element_type=f32)
-        ghs[:, k] = value.astype(bf16).reshape(PLANE, tokens, depth)
-    for tt in range(2):
-        for d in range(PLANE):
-            if tt == 0 and d == 0:
-                continue
-            pp = (p + d) % PLANE
-            copy = remote(
-                ghs.at[pp],
-                gho.at[p, t],
-                h_send.at[tt, d],
-                h_recv.at[p, t],
-                at_plane(pp),
-                (t + tt) % 2,
-            )
-            copy.start()
-            sends.append(copy)
     gho[p, t] = ghs[p]
-    gwown[...] = weight_part(z)
-    for tt in range(2):
-        for d in range(PLANE):
-            if tt == 0 and d == 0:
-                continue
-            src_t, src_p = (t + tt) % 2, (p + d) % PLANE
-            slot = gho.at[src_p, src_t]
-            remote(
-                slot, slot, h_send.at[tt, d], h_recv.at[src_p, src_t], at_plane(src_p), src_t
-            ).wait_recv()
+    for g in range(kv_heads):
+        gwown[g] = weight_part(g, z)
+    for tt, d in plane_peers():
+        src_t, src_p = (t + tt) % 2, (p + d) % PLANE
+        slot = gho.at[src_p, src_t]
+        remote(
+            slot, slot, h_send.at[tt, d], h_recv.at[src_p, src_t], at_plane(src_p), src_t
+        ).wait_recv()
     for zz in range(cols):
         for pp in range(PLANE):
             block = (zz * PLANE + pp) * depth
             gh_out[:, block : block + depth] = gho[pp, zz // per_tp, zz % per_tp]
-    total = gwown[...]
-    for d in range(1, cols):
-        slot = gwr.at[d]
-        remote(slot, slot, g_send.at[d], g_recv.at[d], ((z + d) % cols) * PLANE + p, t).wait_recv()
-        total = total + gwr[d].astype(f32)
-    gwk_out[...] = total[:, :half]
-    gwv_out[...] = total[:, half:]
+    for g in range(kv_heads):
+        total = gwown[g]
+        for d in range(1, cols):
+            slot = gwr.at[g, d]
+            remote(slot, slot, g_send.at[g, d], g_recv.at[g, d], column(d), t).wait_recv()
+            total = total + gwr[g, d].astype(f32)
+        lanes = slice(g * HEAD_SIZE, (g + 1) * HEAD_SIZE)
+        gwk_out[:, lanes] = total[:, :HEAD_SIZE]
+        gwv_out[:, lanes] = total[:, HEAD_SIZE:]
     for copy in sends:
         copy.wait_send()
-    for d in range(1, SPAN):
-
-        @pl.when(j + d < SPAN)
-        def _():
-            kv_copy(d).wait_send()
-
-        @pl.when(j >= d)
-        def _():
-            grad_copy(d).wait_send()
+    for g in range(kv_heads):
+        for d in range(1, SPAN):
+
+            @pl.when(j + d < SPAN)
+            def _():
+                kv_copy(g, d).wait_send()
+
+            @pl.when(j >= d)
+            def _():
+                grad_copy(g, d).wait_send()
 
 
 def fused_device(hidden_states, query, attention_output_gradient, key_weight, value_weight, doc_start):
@@ -592,7 +620,7 @@
     kv_heads = half // HEAD_SIZE
     q_per_kv = query.shape[1] // half
     stack = q_per_kv * tokens
-    pair = 2 * half
+    pair = 2 * HEAD_SIZE
     bf16, f32 = jnp.bfloat16, jnp.float32
     starts = jnp.broadcast_to(doc_start[None, :], (8, tokens))[:1]
     dma = pltpu.SemaphoreType.DMA
@@ -610,41 +638,41 @@
         out_specs=(spec,) * 4,
         scratch_shapes=[
             vmem((cols, PLANE, tokens, depth), bf16),
-            vmem((cols, depth, pair), bf16),
-            vmem((per_tp, depth, pair), bf16),
-            vmem((PLANE, tokens, pair), f32),
-            vmem((PLANE, tokens, pair), f32),
-            vmem((SPAN, tokens, pair), bf16),
+            vmem((kv_heads, cols, depth, pair), bf16),
+            vmem((kv_heads, per_tp, depth, pair), bf16),
+            vmem((kv_heads, PLANE, tokens, pair), f32),
+            vmem((kv_heads, PLANE, tokens, pair), f32),
+            vmem((kv_heads, SPAN, tokens, pair), bf16),
             vmem((kv_heads, stack, HEAD_SIZE), bf16),
             vmem((kv_heads, stack, HEAD_SIZE), bf16),
             vmem((SPAN, tokens, stack), f32),
             vmem((SPAN, tokens, stack), f32),
             vmem((HEAD_SIZE, stack), f32),
-            vmem((SPAN, tokens, pair), f32),
-            vmem((SPAN, tokens, pair), bf16),
-            vmem((SPAN, tokens, pair), bf16),
-            vmem((2, PLANE, tokens, pair), bf16),
-            vmem((depth, pair), f32),
-            vmem((cols, depth, pair), bf16),
-            vmem((cols, depth, pair), bf16),
+            vmem((kv_heads, SPAN, tokens, pair), f32),
+            vmem((kv_heads, SPAN, tokens, pair), bf16),
+            vmem((kv_heads, SPAN, tokens, pair), bf16),
+            vmem((2, kv_heads, PLANE, tokens, pair), bf16),
+            vmem((kv_heads, depth, pair), f32),
+            vmem((kv_heads, cols, depth, pair), bf16),
+            vmem((kv_heads, cols, depth, pair), bf16),
             vmem((PLANE, per_tp, tokens, depth), bf16),
             vmem((PLANE, 2, per_tp, tokens, depth), bf16),
             dma((2, PLANE, per_tp)),
             dma((2, PLANE, per_tp)),
-            dma((cols,)),
-            dma((cols,)),
-            dma((per_tp,)),
-            dma((per_tp,)),
-            dma((PLANE,)),
-            dma((PLANE,)),
-            dma((SPAN,)),
-            dma((SPAN,)),
-            dma((SPAN,)),
-            dma((SPAN,)),
-            dma((2, PLANE)),
-            dma((2, PLANE)),
-            dma((cols,)),
-            dma((cols,)),
+            dma((kv_heads, cols)),
+            dma((kv_heads, cols)),
+            dma((kv_heads, per_tp)),
+            dma((kv_heads, per_tp)),
+            dma((kv_heads, PLANE)),
+            dma((kv_heads, PLANE)),
+            dma((kv_heads, SPAN)),
+            dma((kv_heads, SPAN)),
+            dma((kv_heads, SPAN)),
+            dma((kv_heads, SPAN)),
+            dma((kv_heads, 2, PLANE)),
+            dma((2, kv_heads, PLANE)),
+            dma((kv_heads, cols)),
+            dma((kv_heads, cols)),
             dma((2, PLANE)),
             dma((PLANE, 2)),
         ],

time: 116 us -> 100 us (0.86)
  Pallas kernels: 110 us -> 94.7 us
    pallas_call x1, Pallas kernels: 110 us -> 94.7 us  [fused_device(): pl.pallas_call(functools.partial(exchange_kernel, count_cp, kv_heads, q_p...]
where the time goes in v2:
time: 100 us
  Pallas kernels  94.7 us (95%)
  local copies, waits for them, and re-layouts  4.81 us (5%)
    pallas_call x1, Pallas kernels, fused_device(): pl.pallas_call(functools.partial(exchange_kernel, count_cp, kv_heads, q_p...  94.7 us
    unnamed x10, local copies, waits for them, and re-layouts  4.81 us

profile of v2, /device:TPU:0, one launch (start us, length us, event | category | flops | bytes accessed | tf_op | source)
XLA Modules:
  0.0 100.2 jit_solution(10498152775796998255)
XLA Ops:
  0.6 94.7 %shard_map.93 = (bf16[128,2048]{1,0:T(8,128)(2,1)}, bf16[128,4096]{1,0:T(8,128)(2,1)}, f32[256,256]{1,0:T(8,128)}, f32[256,256]{1,0:T(8,128)}) custom-call(bf16[128,2048]{1,0:T(8,128)(2,1)} %hid.1, bf16[128,2048]{1,0:T(8,128)(2,1)} %qry.1, bf16[128,2048]{1,0:T(8,128)(2,1)} %gout.1, bf16[256,256]{1,0:T(8,128)(2,1)} %wk.1, bf16[256,256]{1,0:T(8,128)(2,1)} %wv.1, ...), custom_call_target="tpu_custom_call" | custom-call | tf_op jit(solution)/shard_map/pallas_call | solution.py:629
  95.3 0.0 copy-start
  95.3 2.0 %copy.14 = bf16[128,2048]{1,0:T(8,128)(2,1)} copy(bf16[128,2048]{1,0:T(8,128)(2,1)} %get-tuple-element.8) | data formatting | bytes 1048576
  97.3 0.0 copy-done
  97.3 0.0 copy-start.2
  97.3 1.0 copy.15
  98.3 0.1 copy-done.2
  98.4 0.0 copy-start.1
  98.4 0.7 copy.16
  99.1 0.3 copy-done.1
  99.5 0.7 copy.17
Async XLA Ops:
  95.3 2.0 %copy-start = (bf16[128,4096]{1,0:T(8,128)(2,1)S(1)}, bf16[128,4096]{1,0:T(8,128)(2,1)}, u32[]{:S(2)}) copy-start(bf16[128,4096]{1,0:T(8,128)(2,1)} %get-tuple-element.9) | copy-start | bytes 3145732
  97.3 1.1 %copy-start.2 = (f32[256,256]{1,0:T(8,128)S(1)}, f32[256,256]{1,0:T(8,128)}, u32[]{:S(2)}) copy-start(f32[256,256]{1,0:T(8,128)} %get-tuple-element.10) | copy-start | bytes 786436
  98.4 1.0 %copy-start.1 = (f32[256,256]{1,0:T(8,128)S(1)}, f32[256,256]{1,0:T(8,128)}, u32[]{:S(2)}) copy-start(f32[256,256]{1,0:T(8,128)} %get-tuple-element.11) | copy-start | bytes 786436

commit v3 on v2

--- a/solution.py
+++ b/solution.py
@@ -345,8 +345,6 @@
             )
             copy.start()
             sends.append(copy)
-    for g in range(1, kv_heads):
-        send_weights(g)
     for k in range(per_tp):
         lane = pl.multiple_of((k * PLANE + p) * depth, HEAD_SIZE)
         xp[t * per_tp + k, p] = hid[:, pl.ds(lane, depth)]
@@ -365,11 +363,14 @@
             ).wait_recv()
 
     def project(g):
+        for d in range(1, cols):
+            zz = (z + d) % cols
+            slot = wz.at[g, zz]
+            remote(slot, slot, w_send.at[g, d], w_recv.at[g, zz], column(d), t).wait_recv()
+        if g < kv_heads - 1:
+            send_weights(g + 1)
         for d in range(cols):
             zz = (z + d) % cols
-            slot = wz.at[g, zz]
-            if d:
-                remote(slot, slot, w_send.at[g, d], w_recv.at[g, zz], column(d), t).wait_recv()
             lhs = xp[zz].reshape(PLANE * tokens, depth)
             add = jnp.dot(lhs, wz[g, zz], preferred_element_type=f32)
             add = add.reshape(PLANE, tokens, pair)
@@ -403,7 +404,7 @@
             remote(slot, slot, r_send.at[g, d], r_recv.at[g, pp], at_plane(pp), t).wait_recv()
             total = total + summed[g, pp]
         kvg[g, j] = total.astype(bf16)
-        for d in range(1, SPAN):
+        for d in reversed(range(1, SPAN)):
 
             @pl.when(j + d < SPAN)
             def _():
@@ -544,10 +545,11 @@
             project(g + 1)
         attend(
             g,
+            nothing,
             functools.partial(finish_keys, g + 1) if g < last else nothing,
-            functools.partial(collect, g - 1) if g else nothing,
         )
         if g:
+            collect(g - 1)
             wait_plane(g - 1, 0)
             send_weight_grads(g - 1)
     collect(last)

time: 100 us -> 93.5 us (0.935)
  Pallas kernels: 94.7 us -> 87.4 us
    pallas_call x1, Pallas kernels: 94.7 us -> 87.4 us  [fused_device(): pl.pallas_call(functools.partial(exchange_kernel, count_cp, kv_heads, q_p...]
where the time goes in v3:
time: 93.5 us; the launch traced here: 92.9 us
  Pallas kernels  87.4 us (93%)
  local copies, waits for them, and re-layouts  4.81 us (5%)
    pallas_call x1, Pallas kernels, fused_device(): pl.pallas_call(functools.partial(exchange_kernel, count_cp, kv_heads, q_p...  87.4 us
    unnamed x10, local copies, waits for them, and re-layouts  4.81 us

profile of v3, /device:TPU:0, one launch (start us, length us, event | category | flops | bytes accessed | tf_op | source)
XLA Modules:
  0.0 92.9 jit_solution(15946814060756311729)
XLA Ops:
  0.6 87.4 %shard_map.93 = (bf16[128,2048]{1,0:T(8,128)(2,1)}, bf16[128,4096]{1,0:T(8,128)(2,1)}, f32[256,256]{1,0:T(8,128)}, f32[256,256]{1,0:T(8,128)}) custom-call(bf16[128,2048]{1,0:T(8,128)(2,1)} %hid.1, bf16[128,2048]{1,0:T(8,128)(2,1)} %qry.1, bf16[128,2048]{1,0:T(8,128)(2,1)} %gout.1, bf16[256,256]{1,0:T(8,128)(2,1)} %wk.1, bf16[256,256]{1,0:T(8,128)(2,1)} %wv.1, ...), custom_call_target="tpu_custom_call" | custom-call | tf_op jit(solution)/shard_map/pallas_call | solution.py:631
  88.0 0.0 copy-start
  88.0 2.0 %copy.14 = bf16[128,2048]{1,0:T(8,128)(2,1)} copy(bf16[128,2048]{1,0:T(8,128)(2,1)} %get-tuple-element.8) | data formatting | bytes 1048576
  90.0 0.0 copy-done
  90.0 0.0 copy-start.2
  90.0 1.0 %copy.15 = bf16[128,4096]{1,0:T(8,128)(2,1)} copy(bf16[128,4096]{1,0:T(8,128)(2,1)S(1)} %copy-done) | data formatting | bytes 2097152
  91.0 0.1 copy-done.2
  91.1 0.0 copy-start.1
  91.1 0.7 copy.16
  91.8 0.3 copy-done.1
  92.2 0.7 copy.17
Async XLA Ops:
  88.0 2.0 %copy-start = (bf16[128,4096]{1,0:T(8,128)(2,1)S(1)}, bf16[128,4096]{1,0:T(8,128)(2,1)}, u32[]{:S(2)}) copy-start(bf16[128,4096]{1,0:T(8,128)(2,1)} %get-tuple-element.9) | copy-start | bytes 3145732
  90.0 1.1 %copy-start.2 = (f32[256,256]{1,0:T(8,128)S(1)}, f32[256,256]{1,0:T(8,128)}, u32[]{:S(2)}) copy-start(f32[256,256]{1,0:T(8,128)} %get-tuple-element.10) | copy-start | bytes 786436
  91.1 1.0 %copy-start.1 = (f32[256,256]{1,0:T(8,128)S(1)}, f32[256,256]{1,0:T(8,128)}, u32[]{:S(2)}) copy-start(f32[256,256]{1,0:T(8,128)} %get-tuple-element.11) | copy-start | bytes 786436
